TPU v7x, 32 devices: a whole 2x2x4 slice. The times are simulated.
32 devices in a mesh: tm: 4 (over y, x), tile: 8 (over z, core).
Axes of the slice: x: 2, y: 2, z: 4, core: 2. Of those that a mesh axis runs over, the one named last changes fastest.
Arguments:
- frame_feats: bfloat16 [4, 64, 128, 1024], P(None, None, 'tile', 'tm'), may hold values from -6 to 6
- send_list: int32 [4, 4, 8, 3, 8], P(None, 'tm', 'tile'), may hold values from 0 to 15
- recv_slot: int32 [4, 4, 8, 16], P(None, 'tm', 'tile'), may hold values from 0 to 23, as said below
- w_unite: bfloat16 [3, 3, 64, 128], replicated, may hold values from -0.1875 to 0.1875
- w_inner: bfloat16 [3, 3, 64, 64], replicated, may hold values from -0.25 to 0.25
- w_outer: bfloat16 [3, 3, 64, 64], replicated, may hold values from -0.25 to 0.25
- w_up: bfloat16 [48, 64], replicated, may hold values from -0.75 to 0.75
Outputs:
- images: bfloat16 [4, 48, 128, 1024], P(None, None, 'tile', 'tm')
Inputs may be any that keep to these rules, and one draw needn't show every extreme that they name: `send_list`: A block index within one band's part of a strip. recv_slot = o*8 + c names entry c of list o of band j + o - 1 in the same strip; band 0 never uses o = 0 and the last band never uses o = 2; for each frame, strip and band, the entries named from one list are 0 .. k-1 with k at most 8, each named once, and some list is named in all 8 entries.
All inputs are finite; a program needn't handle non-finite values.
Results may differ from a plain program's by a relative error of at most 0.019.
Values may be sent and summed in bfloat16 or wider, within the bound.
A program may use at most 64 MiB of HBM per device.

v0:
```python
import functools

import jax
import jax.numpy as jnp
from jax import lax
from jax.experimental import pallas as pl
from jax.experimental.pallas import tpu as pltpu
from jax.sharding import PartitionSpec as P

MESH = pl.DeviceIdType.MESH
HALO = 3
GROUPS = 4
SPAN = 32
LANES = GROUPS * SPAN
bf16 = jnp.bfloat16
f32 = jnp.float32


def lay_taps(taps_ref, matrix):
    kr, kc, out, inp = taps_ref.shape
    for b in range(kc):
        parts = [taps_ref[a, b].astype(f32) for a in range(kr)]
        matrix[b * out : (b + 1) * out] = jnp.concatenate(parts, 1).astype(bf16)


def conv_slab(weights, slab):
    part = jnp.dot(weights, slab, preferred_element_type=f32)
    out, n = part.shape[0] // 3, part.shape[1]
    left = pltpu.roll(part[0:out], 1, 1)
    right = pltpu.roll(part[2 * out : 3 * out], n - 1, 1)
    return left + part[out : 2 * out] + right


def kernel(
    n_tm, n_tile, frames, chan, rows, cols,
    feats_ref, list_ref, slot_ref, tu_ref, ti_ref, to_ref, wp_ref,
    out_ref,
    wu_ref, wi_ref, wo_ref, join, united, inner, state, offer, pool, zone, zone_s, zone_l, zone_r, edge, e_unit, e_inner, e_state, packer, patcher,
    load_sem, fr_send, fr_recv, wr_send, wr_recv, blk_send, blk_recv, zf_send, zf_recv, zw_send, zw_recv,
):
    strip = lax.axis_index("tm")
    band = lax.axis_index("tile")
    has_up, has_down = band > 0, band < n_tile - 1
    has_left, has_right = strip > 0, strip < n_tm - 1
    height, width = n_tile * rows, n_tm * cols
    full = rows + 2 * HALO
    qn = rows // GROUPS + 2 * HALO
    per = rows // GROUPS
    cap = list_ref.shape[4]
    blocks = slot_ref.shape[3]
    entries = cap * rows

    def load(f):
        return pltpu.make_async_copy(
            feats_ref.at[f], join.at[f, pl.ds(HALO, rows), pl.ds(chan, chan), :], load_sem.at[f]
        )

    for f in range(frames):
        load(f).start()

    up, down = {"tile": band - 1}, {"tile": band + 1}
    left, right = {"tm": strip - 1}, {"tm": strip + 1}
    sides = ((has_up, up), (has_down, down), (has_left, left), (has_right, right))

    join[0, :, 0:chan] = jnp.zeros((full, chan, cols), bf16)
    zone[0, :, 0:chan] = jnp.zeros((qn, chan, LANES), bf16)
    zone_l[0, 0:chan] = jnp.zeros((chan, LANES), bf16)
    zone_r[0, 0:chan] = jnp.zeros((chan, LANES), bf16)

    @pl.when(jnp.logical_not(has_up))
    def _():
        join[:, 0:HALO] = jnp.zeros((frames, HALO, 2 * chan, cols), bf16)
        pool[:, 0] = jnp.zeros((frames, rows, chan, entries), bf16)

    @pl.when(jnp.logical_not(has_down))
    def _():
        join[:, HALO + rows : full] = jnp.zeros((frames, HALO, 2 * chan, cols), bf16)
        pool[:, 2] = jnp.zeros((frames, rows, chan, entries), bf16)

    @pl.when(jnp.logical_not(has_left))
    def _():
        zone_l[...] = jnp.zeros(zone_l.shape, bf16)

    @pl.when(jnp.logical_not(has_right))
    def _():
        zone_r[...] = jnp.zeros(zone_r.shape, bf16)

    barrier = pltpu.get_barrier_semaphore()
    for there, device in sides:
        @pl.when(there)
        def _():
            pl.semaphore_signal(barrier, inc=1, device_id=device, device_id_type=MESH)

    lane = lax.broadcasted_iota(jnp.int32, (cols, LANES), 1)
    column = lax.broadcasted_iota(jnp.int32, (cols, LANES), 0)
    inside = lane % SPAN
    half = SPAN // 2
    wanted = jnp.where(
        inside < HALO,
        cols - HALO + inside,
        jnp.where(
            inside < half,
            inside - HALO,
            jnp.where(inside < SPAN - HALO, cols + HALO - SPAN + inside, inside - (SPAN - HALO)),
        ),
    )
    p_lane = lax.broadcasted_iota(jnp.int32, (LANES, cols), 0)
    p_col = lax.broadcasted_iota(jnp.int32, (LANES, cols), 1)
    p_in = p_lane % SPAN
    for g in range(GROUPS):
        packer[g] = ((lane // SPAN == g) & (column == wanted)).astype(f32).astype(bf16)
        here = jnp.where(p_in < half, p_in - HALO, cols + HALO - SPAN + p_in)
        near = (p_col < HALO) | (p_col >= cols - HALO)
        patcher[g] = ((p_lane // SPAN == g) & near & (here == p_col)).astype(f32).astype(bf16)

    pl.semaphore_wait(barrier, sum(there.astype(jnp.int32) for there, _ in sides))

    def remote(src, dst, send, recv, device):
        return pltpu.make_async_remote_copy(
            src_ref=src, dst_ref=dst, send_sem=send, recv_sem=recv, device_id=device, device_id_type=MESH
        )

    def row_pair(f, base, send, recv):
        part = pl.ds(base, chan)
        return (
            (has_up, remote(join.at[f, pl.ds(HALO, HALO), part, :], join.at[f, pl.ds(HALO + rows, HALO), part, :],
                            send.at[f, 0], recv.at[f, 0], up), has_down),
            (has_down, remote(join.at[f, pl.ds(rows, HALO), part, :], join.at[f, pl.ds(0, HALO), part, :],
                              send.at[f, 1], recv.at[f, 1], down), has_up),
        )

    def block_pair(f):
        return (
            (has_down, remote(offer.at[f, 0], pool.at[f, 0],
                              blk_send.at[f, 0], blk_recv.at[f, 0], down), has_up),
            (has_up, remote(offer.at[f, 1], pool.at[f, 2],
                            blk_send.at[f, 1], blk_recv.at[f, 1], up), has_down),
        )

    def zone_pair(f, base, send, recv):
        part = pl.ds(base, chan)
        return (
            (has_right, remote(zone_s.at[f, 0, part, :], zone_l.at[f, part, :],
                               send.at[f, 0], recv.at[f, 0], right), has_left),
            (has_left, remote(zone_s.at[f, 1, part, :], zone_r.at[f, part, :],
                              send.at[f, 1], recv.at[f, 1], left), has_right),
        )

    def start(pair):
        for sends, copy, _ in pair:
            pl.when(sends)(copy.start)

    def arrive(pair):
        for _, copy, gets in pair:
            pl.when(gets)(copy.wait_recv)

    def sent(pair):
        for sends, copy, _ in pair:
            pl.when(sends)(copy.wait_send)

    e_lane = lax.broadcasted_iota(jnp.int32, (1, LANES), 1)
    e_in = e_lane % SPAN

    def pack_zone(f, base):
        total = jnp.zeros((qn * chan, LANES), f32)
        for g in range(GROUPS):
            part = join[f, per * g : per * g + qn, base : base + chan, :].reshape(qn * chan, cols)
            total = total + jnp.dot(part, packer[g], preferred_element_type=f32)
        total = total.reshape(qn, chan, LANES)
        zone[f, :, base : base + chan, :] = total.astype(bf16)
        last, first = total[0], pltpu.roll(total[0], LANES - (SPAN - HALO), 1)
        for q in range(1, qn):
            here = (e_in >= HALO * q) & (e_in < HALO * (q + 1))
            last = jnp.where(here, pltpu.roll(total[q], HALO * q, 1), last)
            first = jnp.where(here, pltpu.roll(total[q], (LANES - (SPAN - HALO) + HALO * q) % LANES, 1), first)
        zone_s[f, 0, base : base + chan, :] = last.astype(bf16)
        zone_s[f, 1, base : base + chan, :] = first.astype(bf16)

    for f in range(frames):
        load(f).wait()
        start(row_pair(f, chan, fr_send, fr_recv))

    lay_taps(tu_ref, wu_ref)
    lay_taps(ti_ref, wi_ref)
    lay_taps(to_ref, wo_ref)

    e_col = strip * cols + jnp.where(e_in < half, e_in - HALO, cols + HALO - SPAN + e_in)
    col_ok = (e_col >= 0) & (e_col < width)
    e_row = band * rows + per * (e_lane // SPAN) - HALO

    def edge_ok(q):
        row = e_row + q
        return col_ok & (row >= 0) & (row < height)

    def unite_row(f, r):
        return conv_slab(wu_ref[...], join[f, pl.ds(r - 1, 3)].reshape(6 * chan, cols))

    def frame(f, carry):
        arrive(row_pair(f, chan, fr_send, fr_recv))
        pack_zone(f, chan)
        start(zone_pair(f, chan, zf_send, zf_recv))

        @pl.when(f > 0)
        def _():
            arrive(block_pair(f))
            spot = lax.broadcasted_iota(jnp.int32, (1, cols), 1)
            source = jnp.zeros((1, cols), jnp.int32)
            for d in range(blocks):
                source = jnp.where(spot // rows == d, slot_ref[f, 0, 0, d] * rows, source)
            index = lax.broadcasted_iota(jnp.int32, (3 * entries, cols), 0)
            placer = (index == source + spot % rows).astype(f32).astype(bf16)
            whole = jnp.concatenate([pool[f, o].reshape(rows * chan, entries) for o in range(3)], 1)
            warped = jnp.dot(whole, placer, preferred_element_type=f32)
            join[f, HALO : HALO + rows, 0:chan, :] = warped.astype(bf16).reshape(rows, chan, cols)
            start(row_pair(f, 0, wr_send, wr_recv))

        for r in range(HALO + 1, HALO + rows - 1):
            united[r] = unite_row(f, r).astype(bf16)

        @pl.when(f > 0)
        def _():
            arrive(row_pair(f, 0, wr_send, wr_recv))
            pack_zone(f, 0)
            start(zone_pair(f, 0, zw_send, zw_recv))

        for r in (1, 2, HALO):
            value = unite_row(f, r)
            united[r] = (value if r == HALO else jnp.where(has_up, value, 0.0)).astype(bf16)
        for r in (HALO + rows - 1, HALO + rows, HALO + rows + 1):
            value = unite_row(f, r)
            united[r] = (value if r < HALO + rows else jnp.where(has_down, value, 0.0)).astype(bf16)

        def inner_row(r):
            slab = united[pl.ds(r - 1, 3)].reshape(3 * chan, cols)
            return jnp.maximum(conv_slab(wi_ref[...], slab), 0.0)

        for r in range(HALO, HALO + rows):
            inner[r] = inner_row(r).astype(bf16)
        inner[2] = jnp.where(has_up, inner_row(2), 0.0).astype(bf16)
        inner[HALO + rows] = jnp.where(has_down, inner_row(HALO + rows), 0.0).astype(bf16)

        def outer_row(r):
            slab = inner[pl.ds(r - 1, 3)].reshape(3 * chan, cols)
            state[r - HALO] = (united[r].astype(f32) + conv_slab(wo_ref[...], slab)).astype(bf16)

        for r in range(HALO, HALO + rows):
            outer_row(r)

        arrive(zone_pair(f, chan, zf_send, zf_recv))

        @pl.when(f > 0)
        def _():
            arrive(zone_pair(f, 0, zw_send, zw_recv))

        from_l, from_r = zone_l[f].astype(f32), zone_r[f].astype(f32)
        for q in range(qn):
            before = pltpu.roll(from_l, (LANES - HALO * q) % LANES, 1)
            after = pltpu.roll(from_r, (LANES + SPAN - HALO - HALO * q) % LANES, 1)
            value = jnp.where(e_in < HALO, before, jnp.where(e_in >= SPAN - HALO, after, zone[f, q].astype(f32)))
            edge[q] = value.astype(bf16)
        for q in range(1, qn - 1):
            value = conv_slab(wu_ref[...], edge[q - 1 : q + 2].reshape(6 * chan, LANES))
            e_unit[q] = jnp.where(edge_ok(q), value, 0.0).astype(bf16)
        for q in range(2, qn - 2):
            value = conv_slab(wi_ref[...], e_unit[q - 1 : q + 2].reshape(3 * chan, LANES))
            e_inner[q] = jnp.where(edge_ok(q), jnp.maximum(value, 0.0), 0.0).astype(bf16)
        for q in range(3, qn - 3):
            value = conv_slab(wo_ref[...], e_inner[q - 1 : q + 2].reshape(3 * chan, LANES))
            e_state[q - 3] = (e_unit[q].astype(f32) + value).astype(bf16)

        ends = e_state[...].reshape(per * chan, LANES)
        spot = lax.broadcasted_iota(jnp.int32, (per * chan, cols), 1)
        near = (spot < HALO) | (spot >= cols - HALO)
        for g in range(GROUPS):
            patch = jnp.dot(ends, patcher[g], preferred_element_type=f32)
            old = state[per * g : per * (g + 1)].reshape(per * chan, cols).astype(f32)
            state[per * g : per * (g + 1)] = jnp.where(near, patch, old).astype(bf16).reshape(per, chan, cols)

        @pl.when(f < frames - 1)
        def _():
            spot = lax.broadcasted_iota(jnp.int32, (1, entries), 1)
            index = lax.broadcasted_iota(jnp.int32, (cols, entries), 0)
            whole = state[...].reshape(rows * chan, cols)
            pickers = []
            for o in (0, 2, 1):
                target = jnp.zeros((1, entries), jnp.int32)
                for c in range(cap):
                    target = jnp.where(spot // rows == c, list_ref[f + 1, 0, 0, o, c] * rows, target)
                pickers.append((index == target + spot % rows).astype(f32).astype(bf16))
            away = jnp.dot(whole, jnp.concatenate(pickers[:2], 1), preferred_element_type=f32).astype(bf16)
            offer[f + 1, 0] = away[:, :entries].reshape(rows, chan, entries)
            offer[f + 1, 1] = away[:, entries:].reshape(rows, chan, entries)
            start(block_pair(f + 1))
            kept = jnp.dot(whole, pickers[2], preferred_element_type=f32).astype(bf16)
            pool[f + 1, 1] = kept.reshape(rows, chan, entries)

        for r in range(rows):
            out_ref[f, r] = jnp.dot(wp_ref[...], state[r], preferred_element_type=f32).astype(bf16)

        sent(row_pair(f, chan, fr_send, fr_recv))
        sent(zone_pair(f, chan, zf_send, zf_recv))

        @pl.when(f > 0)
        def _():
            sent(row_pair(f, 0, wr_send, wr_recv))
            sent(zone_pair(f, 0, zw_send, zw_recv))
            sent(block_pair(f))

        return carry

    lax.fori_loop(0, frames, frame, 0)


def on_device(n_tm, n_tile, frame_feats, send_list, recv_slot, w_unite, w_inner, w_outer, w_up):
    frames, chan, rows, cols = frame_feats.shape
    planes = w_up.shape[0]
    feats = frame_feats.transpose(0, 2, 1, 3)
    entries = send_list.shape[4] * rows
    full = rows + 2 * HALO
    per = rows // GROUPS
    qn = per + 2 * HALO
    vmem = pl.BlockSpec(memory_space=pltpu.VMEM)
    smem = pl.BlockSpec(memory_space=pltpu.SMEM)
    sems = pltpu.SemaphoreType.DMA((frames, 2))
    out = pl.pallas_call(
        functools.partial(kernel, n_tm, n_tile, frames, chan, rows, cols),
        out_shape=jax.ShapeDtypeStruct((frames, rows, planes, cols), bf16),
        in_specs=[pl.BlockSpec(memory_space=pl.ANY)] + [smem] * 2 + [vmem] * 4,
        out_specs=vmem,
        scratch_shapes=[
            pltpu.VMEM((3 * chan, 6 * chan), bf16),
            pltpu.VMEM((3 * chan, 3 * chan), bf16),
            pltpu.VMEM((3 * chan, 3 * chan), bf16),
            pltpu.VMEM((frames, full, 2 * chan, cols), bf16),
            pltpu.VMEM((full, chan, cols), bf16),
            pltpu.VMEM((full, chan, cols), bf16),
            pltpu.VMEM((rows, chan, cols), bf16),
            pltpu.VMEM((frames, 2, rows, chan, entries), bf16),
            pltpu.VMEM((frames, 3, rows, chan, entries), bf16),
            pltpu.VMEM((frames, qn, 2 * chan, LANES), bf16),
            pltpu.VMEM((frames, 2, 2 * chan, LANES), bf16),
            pltpu.VMEM((frames, 2 * chan, LANES), bf16),
            pltpu.VMEM((frames, 2 * chan, LANES), bf16),
            pltpu.VMEM((qn, 2 * chan, LANES), bf16),
            pltpu.VMEM((qn, chan, LANES), bf16),
            pltpu.VMEM((qn, chan, LANES), bf16),
            pltpu.VMEM((per, chan, LANES), bf16),
            pltpu.VMEM((GROUPS, cols, LANES), bf16),
            pltpu.VMEM((GROUPS, LANES, cols), bf16),
            pltpu.SemaphoreType.DMA((frames,)),
        ] + [sems] * 10,
        compiler_params=pltpu.CompilerParams(
            collective_id=0, has_side_effects=True, vmem_limit_bytes=48 * 1024 * 1024
        ),
        name="propagate",
    )(feats, send_list, recv_slot, w_unite, w_inner, w_outer, w_up)
    return out.transpose(0, 2, 1, 3)


def solution(mesh):
    placed = (
        P(None, None, "tile", "tm"),
        P(None, "tm", "tile", None, None),
        P(None, "tm", "tile", None),
        P(),
        P(),
        P(),
        P(),
    )
    return jax.shard_map(
        functools.partial(on_device, mesh.shape["tm"], mesh.shape["tile"]),
        mesh=mesh,
        in_specs=placed,
        out_specs=P(None, None, "tile", "tm"),
        check_vma=False,
    )
```

profile of v0, /device:TPU:1, one launch (start us, length us, event | category | flops | bytes accessed | tf_op | source)
XLA Modules:
  0.0 58.9 jit_solution(13406052199318657987)
XLA Ops:
  0.0 0.7 %copy.9.list_ref = s32[4,1,1,3,8]{4,3,2,1,0:T(4,128)S(1)} copy(s32[4,1,1,3,8]{4,2,3,1,0:T(1,128)} %param.8) | data formatting | bytes 768 | tf_op args[1]
  0.7 0.0 copy-start
  0.7 0.0 copy-start.1
  0.7 0.0 copy-start.2
  0.7 0.0 copy-start.3
  0.7 0.0 copy-start.4
  0.7 2.4 %copy.12 = bf16[4,64,16,256]{3,1,2,0:T(8,128)(2,1)S(1)} copy(bf16[4,64,16,256]{3,2,1,0:T(8,128)(2,1)} %param.7) | data formatting | bytes 4194304 | tf_op args[0]
  3.1 0.0 copy-done
  3.2 0.0 copy-done.1
  3.2 0.0 copy-done.2
  3.2 0.0 copy-done.3
  3.2 0.0 copy-done.4
  3.2 54.0 %propagate.1 = bf16[4,16,48,256]{3,2,1,0:T(8,128)(2,1)S(1)} custom-call(bf16[4,16,64,256]{3,2,1,0:T(8,128)(2,1)S(1)} %bitcast.4, s32[4,1,1,3,8]{4,3,2,1,0:T(4,128)S(1)} %copy.9.list_ref, s32[4,1,1,16]{3,2,1,0:T(1,128)S(1)} %copy-done.4, bf16[3,3,64,128]{3,2,1,0:T(8,128)(2,1)S(1)} %copy-done, bf16[3,3,64,64]{3,2,1,0:T(8,128)(2,1)S(1)} %copy-done.1, ...), custom_call_target="tpu_custom_call" | custom-call | tf_op jit(solution)/shard_map/propagate/pallas_call | solution.py:325
  57.2 1.7 %copy.10 = bf16[4,48,16,256]{3,2,1,0:T(8,128)(2,1)} copy(bf16[4,48,16,256]{3,1,2,0:T(8,128)(2,1)S(1)} %bitcast.5) | data formatting | bytes 3145728 | tf_op jit(solution)/shard_map/transpose | solution.py:357
Async XLA Ops:
  0.7 2.4 %copy-start = (bf16[3,3,64,128]{3,2,1,0:T(8,128)(2,1)S(1)}, bf16[3,3,64,128]{3,2,1,0:T(8,128)(2,1)}, u32[]{:S(2)}) copy-start(bf16[3,3,64,128]{3,2,1,0:T(8,128)(2,1)} %tu_ref.1) | copy-start | bytes 442372
  0.7 2.5 %copy-start.1 = (bf16[3,3,64,64]{3,2,1,0:T(8,128)(2,1)S(1)}, bf16[3,3,64,64]{3,2,1,0:T(8,128)(2,1)}, u32[]{:S(2)}) copy-start(bf16[3,3,64,64]{3,2,1,0:T(8,128)(2,1)} %ti_ref.1) | copy-start | bytes 221188
  0.7 2.5 %copy-start.2 = (bf16[3,3,64,64]{3,2,1,0:T(8,128)(2,1)S(1)}, bf16[3,3,64,64]{3,2,1,0:T(8,128)(2,1)}, u32[]{:S(2)}) copy-start(bf16[3,3,64,64]{3,2,1,0:T(8,128)(2,1)} %to_ref.1) | copy-start | bytes 221188
  0.7 2.5 %copy-start.3 = (bf16[48,64]{1,0:T(8,128)(2,1)S(1)}, bf16[48,64]{1,0:T(8,128)(2,1)}, u32[]{:S(2)}) copy-start(bf16[48,64]{1,0:T(8,128)(2,1)} %wp_ref.1) | copy-start | bytes 18436
  0.7 2.5 %copy-start.4 = (s32[4,1,1,16]{3,2,1,0:T(1,128)S(1)}, s32[4,1,1,16]{3,2,1,0:T(1,128)}, u32[]{:S(2)}) copy-start(s32[4,1,1,16]{3,2,1,0:T(1,128)} %slot_ref.1) | copy-start | bytes 772
where the time goes:
time: 59.6 us; the launch traced here: 58.9 us
  Pallas kernels  54 us (91%)
  local copies, waits for them, and re-layouts  4.82 us (8%)
    pallas_call x1, Pallas kernels, on_device(): pl.pallas_call(functools.partial(kernel, n_tm, n_tile, frames, chan, rows...  54 us
    unnamed x12, local copies, waits for them, and re-layouts  3.13 us
    transpose x1, local copies, waits for them, and re-layouts, on_device(): return out.transpose(0, 2, 1, 3)  1.69 us

commit v1 on v0

v1 whole, which is shorter than its diff:
```python
import functools

import jax
import jax.numpy as jnp
from jax import lax
from jax.experimental import pallas as pl
from jax.experimental.pallas import tpu as pltpu
from jax.sharding import PartitionSpec as P

MESH = pl.DeviceIdType.MESH
HALO = 3
GROUPS = 4
SPAN = 32
LANES = GROUPS * SPAN
PIECES = 2
bf16 = jnp.bfloat16
f32 = jnp.float32


def lay_taps(taps_ref, base, matrix):
    kr, kc, out, _ = taps_ref.shape
    inp = matrix.shape[1] // (kr + 1)
    blank = jnp.zeros((out, inp), f32)
    for p in range(2):
        for b in range(kc):
            parts = []
            for a in range(kr + 1):
                tap = a - p
                parts.append(taps_ref[tap, b][:, base : base + inp].astype(f32) if 0 <= tap < kr else blank)
            row = (p * kc + b) * out
            matrix[row : row + out] = jnp.concatenate(parts, 1).astype(bf16)


def conv_pair(weights, slab):
    part = jnp.dot(weights, slab, preferred_element_type=f32)
    out, n = part.shape[0] // 6, part.shape[1]
    rows = []
    for p in range(2):
        base = 3 * out * p
        left = pltpu.roll(part[base : base + out], 1, 1)
        right = pltpu.roll(part[base + 2 * out : base + 3 * out], n - 1, 1)
        rows.append(left + part[base + out : base + 2 * out] + right)
    return rows


def kernel(
    n_tm, n_tile, frames, chan, rows, cols,
    feats_ref, list_ref, slot_ref, tu_ref, ti_ref, to_ref, wp_ref,
    out_ref,
    ww_ref, wf_ref, wi_ref, wo_ref, feats, warped, partial, united, inner, state, offer, pool,
    zone_s, zone_r, zone_f, zone_w, edge, e_part, e_unit, e_inner, e_state, packer, patcher,
    load_sem, row_send, row_recv, blk_send, blk_recv, zone_send, zone_recv,
):
    strip = lax.axis_index("tm")
    band = lax.axis_index("tile")
    has_up, has_down = band > 0, band < n_tile - 1
    has_left, has_right = strip > 0, strip < n_tm - 1
    height, width = n_tile * rows, n_tm * cols
    full = rows + 2 * HALO
    per = rows // GROUPS
    qn = per + 2 * HALO
    cap = list_ref.shape[4]
    blocks = slot_ref.shape[3]
    entries = cap * rows
    piece = rows // PIECES

    def load(f):
        return pltpu.make_async_copy(feats_ref.at[f], feats.at[f, pl.ds(HALO, rows)], load_sem.at[f])

    for f in range(frames):
        load(f).start()

    up, down = {"tile": band - 1}, {"tile": band + 1}
    left, right = {"tm": strip - 1}, {"tm": strip + 1}
    sides = ((has_up, up), (has_down, down), (has_left, left), (has_right, right))

    @pl.when(jnp.logical_not(has_up))
    def _():
        feats[:, 0:HALO] = jnp.zeros((frames, HALO, chan, cols), bf16)
        warped[:, 0:HALO] = jnp.zeros((frames, HALO, chan, cols), bf16)
        pool[:, 0] = jnp.zeros((frames, rows, chan, entries), bf16)

    @pl.when(jnp.logical_not(has_down))
    def _():
        feats[:, HALO + rows : full] = jnp.zeros((frames, HALO, chan, cols), bf16)
        warped[:, HALO + rows : full] = jnp.zeros((frames, HALO, chan, cols), bf16)
        pool[:, 2] = jnp.zeros((frames, rows, chan, entries), bf16)

    @pl.when(jnp.logical_not(has_left))
    def _():
        zone_r[:, :, 0] = jnp.zeros((frames, 2, chan, LANES), bf16)

    @pl.when(jnp.logical_not(has_right))
    def _():
        zone_r[:, :, 1] = jnp.zeros((frames, 2, chan, LANES), bf16)

    barrier = pltpu.get_barrier_semaphore()
    for there, device in sides:
        @pl.when(there)
        def _():
            pl.semaphore_signal(barrier, inc=1, device_id=device, device_id_type=MESH)

    lane = lax.broadcasted_iota(jnp.int32, (cols, LANES), 1)
    column = lax.broadcasted_iota(jnp.int32, (cols, LANES), 0)
    inside = lane % SPAN
    half = SPAN // 2
    wanted = jnp.where(
        inside < HALO,
        cols - HALO + inside,
        jnp.where(
            inside < half,
            inside - HALO,
            jnp.where(inside < SPAN - HALO, cols + HALO - SPAN + inside, inside - (SPAN - HALO)),
        ),
    )
    p_lane = lax.broadcasted_iota(jnp.int32, (LANES, cols), 0)
    p_col = lax.broadcasted_iota(jnp.int32, (LANES, cols), 1)
    p_in = p_lane % SPAN
    for g in range(GROUPS):
        packer[g] = ((lane // SPAN == g) & (column == wanted)).astype(f32).astype(bf16)
        here = jnp.where(p_in < half, p_in - HALO, cols + HALO - SPAN + p_in)
        near = (p_col < HALO) | (p_col >= cols - HALO)
        patcher[g] = ((p_lane // SPAN == g) & near & (here == p_col)).astype(f32).astype(bf16)

    for f in range(frames):
        load(f).wait()

    pl.semaphore_wait(barrier, sum(there.astype(jnp.int32) for there, _ in sides))

    def remote(src, dst, send, recv, device):
        return pltpu.make_async_remote_copy(
            src_ref=src, dst_ref=dst, send_sem=send, recv_sem=recv, device_id=device, device_id_type=MESH
        )

    def row_pair(f, kind, ref):
        return (
            (has_up, remote(ref.at[f, pl.ds(HALO, HALO)], ref.at[f, pl.ds(HALO + rows, HALO)],
                            row_send.at[f, kind, 0], row_recv.at[f, kind, 0], up), has_down),
            (has_down, remote(ref.at[f, pl.ds(rows, HALO)], ref.at[f, pl.ds(0, HALO)],
                              row_send.at[f, kind, 1], row_recv.at[f, kind, 1], down), has_up),
        )

    def block_pair(f, h):
        part = pl.ds(piece * h, piece)
        return (
            (has_down, remote(offer.at[f, 0, part], pool.at[f, 0, part],
                              blk_send.at[f, h, 0], blk_recv.at[f, h, 0], down), has_up),
            (has_up, remote(offer.at[f, 1, part], pool.at[f, 2, part],
                            blk_send.at[f, h, 1], blk_recv.at[f, h, 1], up), has_down),
        )

    def zone_pair(f, kind):
        return (
            (has_right, remote(zone_s.at[f, kind, 0], zone_r.at[f, kind, 0],
                               zone_send.at[f, kind, 0], zone_recv.at[f, kind, 0], right), has_left),
            (has_left, remote(zone_s.at[f, kind, 1], zone_r.at[f, kind, 1],
                              zone_send.at[f, kind, 1], zone_recv.at[f, kind, 1], left), has_right),
        )

    def start(pair):
        for sends, copy, _ in pair:
            pl.when(sends)(copy.start)

    def arrive(pair):
        for _, copy, gets in pair:
            pl.when(gets)(copy.wait_recv)

    def sent(pair):
        for sends, copy, _ in pair:
            pl.when(sends)(copy.wait_send)

    for f in range(frames):
        start(row_pair(f, 0, feats))
    lay_taps(tu_ref, 0, ww_ref)
    lay_taps(tu_ref, chan, wf_ref)
    lay_taps(ti_ref, 0, wi_ref)
    lay_taps(to_ref, 0, wo_ref)

    e_lane = lax.broadcasted_iota(jnp.int32, (1, LANES), 1)
    e_in = e_lane % SPAN
    e_col = strip * cols + jnp.where(e_in < half, e_in - HALO, cols + HALO - SPAN + e_in)
    col_ok = (e_col >= 0) & (e_col < width)
    e_row = band * rows + per * (e_lane // SPAN) - HALO

    def edge_ok(q):
        row = e_row + q
        return col_ok & (row >= 0) & (row < height)

    def pack_zone(f, kind, ref, zone):
        total = jnp.zeros((qn * chan, LANES), f32)
        for g in range(GROUPS):
            part = ref[f, per * g : per * g + qn].reshape(qn * chan, cols)
            total = total + jnp.dot(part, packer[g], preferred_element_type=f32)
        total = total.reshape(qn, chan, LANES)
        zone[...] = total.astype(bf16)
        last, first = total[0], pltpu.roll(total[0], LANES - (SPAN - HALO), 1)
        for q in range(1, qn):
            here = (e_in >= HALO * q) & (e_in < HALO * (q + 1))
            last = jnp.where(here, pltpu.roll(total[q], HALO * q, 1), last)
            first = jnp.where(here, pltpu.roll(total[q], (LANES - (SPAN - HALO) + HALO * q) % LANES, 1), first)
        zone_s[f, kind, 0] = last.astype(bf16)
        zone_s[f, kind, 1] = first.astype(bf16)
        start(zone_pair(f, kind))

    def lay_edge(f, kind, zone):
        arrive(zone_pair(f, kind))
        from_l, from_r = zone_r[f, kind, 0].astype(f32), zone_r[f, kind, 1].astype(f32)
        for q in range(qn):
            before = pltpu.roll(from_l, (LANES - HALO * q) % LANES, 1)
            after = pltpu.roll(from_r, (LANES + SPAN - HALO - HALO * q) % LANES, 1)
            value = jnp.where(e_in < HALO, before, jnp.where(e_in >= SPAN - HALO, after, zone[q].astype(f32)))
            edge[q] = value.astype(bf16)

    def inside_rows(r, value):
        if r < HALO:
            return jnp.where(has_up, value, 0.0).astype(bf16)
        if r >= HALO + rows:
            return jnp.where(has_down, value, 0.0).astype(bf16)
        return value.astype(bf16)

    def unite(f, r):
        pair = conv_pair(ww_ref[...], warped[f, r - 1 : r + 3].reshape(4 * chan, cols))
        for p in range(2):
            united[r + p] = inside_rows(r + p, pair[p] + partial[r + p])

    def inner_pair(r):
        pair = conv_pair(wi_ref[...], united[r - 1 : r + 3].reshape(4 * chan, cols))
        for p in range(2):
            inner[r + p] = inside_rows(r + p, jnp.maximum(pair[p], 0.0))

    def outer_pair(r):
        pair = conv_pair(wo_ref[...], inner[r - 1 : r + 3].reshape(4 * chan, cols))
        for p in range(2):
            state[r + p - HALO] = (united[r + p].astype(f32) + pair[p]).astype(bf16)

    def inner_middle():
        for r in range(6, rows, 2):
            inner_pair(r)

    def frame(f, carry):
        arrive(row_pair(f, 0, feats))
        pack_zone(f, 0, feats, zone_f)
        for r in range(1, full - 1, 2):
            pair = conv_pair(wf_ref[...], feats[f, r - 1 : r + 3].reshape(4 * chan, cols))
            partial[r], partial[r + 1] = pair
        lay_edge(f, 0, zone_f)
        for q in range(1, qn - 1, 2):
            pair = conv_pair(wf_ref[...], edge[q - 1 : q + 3].reshape(4 * chan, LANES))
            e_part[q], e_part[q + 1] = pair

        @pl.when(f == 0)
        def _():
            for r in range(1, full - 1):
                united[r] = inside_rows(r, partial[r])
            inner_middle()

        @pl.when(f > 0)
        def _():
            spot = lax.broadcasted_iota(jnp.int32, (1, cols), 1)
            source = jnp.zeros((1, cols), jnp.int32)
            for d in range(blocks):
                source = jnp.where(spot // rows == d, slot_ref[f, 0, 0, d] * rows, source)
            index = lax.broadcasted_iota(jnp.int32, (3 * entries, cols), 0)
            placer = (index == source + spot % rows).astype(f32).astype(bf16)
            for h in range(PIECES):
                arrive(block_pair(f, h))
                part = slice(piece * h, piece * (h + 1))
                whole = jnp.concatenate([pool[f, o, part].reshape(piece * chan, entries) for o in range(3)], 1)
                placed = jnp.dot(whole, placer, preferred_element_type=f32).astype(bf16)
                warped[f, HALO + piece * h : HALO + piece * (h + 1)] = placed.reshape(piece, chan, cols)
                if h == 0:
                    start(row_pair(f, 1, warped)[:1])
            start(row_pair(f, 1, warped)[1:])
            for r in range(5, rows, 2):
                unite(f, r)
            inner_middle()
            arrive(row_pair(f, 1, warped))
            pack_zone(f, 1, warped, zone_w)
            for r in (1, 3, rows + 1, rows + 3):
                unite(f, r)

        for r in (2, 4, rows, rows + 2):
            inner_pair(r)
        for r in range(HALO, HALO + rows, 2):
            outer_pair(r)

        @pl.when(f == 0)
        def _():
            for q in range(1, qn - 1):
                e_unit[q] = jnp.where(edge_ok(q), e_part[q], 0.0).astype(bf16)

        @pl.when(f > 0)
        def _():
            lay_edge(f, 1, zone_w)
            for q in range(1, qn - 1, 2):
                pair = conv_pair(ww_ref[...], edge[q - 1 : q + 3].reshape(4 * chan, LANES))
                for p in range(2):
                    e_unit[q + p] = jnp.where(edge_ok(q + p), pair[p] + e_part[q + p], 0.0).astype(bf16)

        for q in range(2, qn - 2, 2):
            pair = conv_pair(wi_ref[...], e_unit[q - 1 : q + 3].reshape(4 * chan, LANES))
            for p in range(2):
                e_inner[q + p] = jnp.where(edge_ok(q + p), jnp.maximum(pair[p], 0.0), 0.0).astype(bf16)
        for q in range(3, qn - 3, 2):
            pair = conv_pair(wo_ref[...], e_inner[q - 1 : q + 3].reshape(4 * chan, LANES))
            for p in range(2):
                e_state[q + p - 3] = (e_unit[q + p].astype(f32) + pair[p]).astype(bf16)

        ends = e_state[...].reshape(per * chan, LANES)
        spot = lax.broadcasted_iota(jnp.int32, (per * chan, cols), 1)
        near = (spot < HALO) | (spot >= cols - HALO)
        for g in range(GROUPS):
            patch = jnp.dot(ends, patcher[g], preferred_element_type=f32)
            old = state[per * g : per * (g + 1)].reshape(per * chan, cols).astype(f32)
            state[per * g : per * (g + 1)] = jnp.where(near, patch, old).astype(bf16).reshape(per, chan, cols)

        @pl.when(f < frames - 1)
        def _():
            spot = lax.broadcasted_iota(jnp.int32, (1, entries), 1)
            index = lax.broadcasted_iota(jnp.int32, (cols, entries), 0)
            pickers = []
            for o in (0, 2, 1):
                target = jnp.zeros((1, entries), jnp.int32)
                for c in range(cap):
                    target = jnp.where(spot // rows == c, list_ref[f + 1, 0, 0, o, c] * rows, target)
                pickers.append((index == target + spot % rows).astype(f32).astype(bf16))
            both = jnp.concatenate(pickers[:2], 1)
            for h in range(PIECES):
                part = slice(piece * h, piece * (h + 1))
                whole = state[part].reshape(piece * chan, cols)
                away = jnp.dot(whole, both, preferred_element_type=f32).astype(bf16)
                offer[f + 1, 0, part] = away[:, :entries].reshape(piece, chan, entries)
                offer[f + 1, 1, part] = away[:, entries:].reshape(piece, chan, entries)
                start(block_pair(f + 1, h))
            kept = jnp.dot(state[...].reshape(rows * chan, cols), pickers[2], preferred_element_type=f32)
            pool[f + 1, 1] = kept.astype(bf16).reshape(rows, chan, entries)

        for r in range(rows):
            out_ref[f, r] = jnp.dot(wp_ref[...], state[r], preferred_element_type=f32).astype(bf16)

        sent(row_pair(f, 0, feats))
        sent(zone_pair(f, 0))

        @pl.when(f > 0)
        def _():
            sent(row_pair(f, 1, warped))
            sent(zone_pair(f, 1))
            for h in range(PIECES):
                sent(block_pair(f, h))

        return carry

    lax.fori_loop(0, frames, frame, 0)


def on_device(n_tm, n_tile, frame_feats, send_list, recv_slot, w_unite, w_inner, w_outer, w_up):
    frames, chan, rows, cols = frame_feats.shape
    planes = w_up.shape[0]
    feats = frame_feats.transpose(0, 2, 1, 3)
    entries = send_list.shape[4] * rows
    full = rows + 2 * HALO
    per = rows // GROUPS
    qn = per + 2 * HALO
    vmem = pl.BlockSpec(memory_space=pltpu.VMEM)
    smem = pl.BlockSpec(memory_space=pltpu.SMEM)

    def sems(kinds):
        return pltpu.SemaphoreType.DMA((frames, kinds, 2))

    out = pl.pallas_call(
        functools.partial(kernel, n_tm, n_tile, frames, chan, rows, cols),
        out_shape=jax.ShapeDtypeStruct((frames, rows, planes, cols), bf16),
        in_specs=[pl.BlockSpec(memory_space=pl.ANY)] + [smem] * 2 + [vmem] * 4,
        out_specs=vmem,
        scratch_shapes=[
            pltpu.VMEM((6 * chan, 4 * chan), bf16),
            pltpu.VMEM((6 * chan, 4 * chan), bf16),
            pltpu.VMEM((6 * chan, 4 * chan), bf16),
            pltpu.VMEM((6 * chan, 4 * chan), bf16),
            pltpu.VMEM((frames, full, chan, cols), bf16),
            pltpu.VMEM((frames, full, chan, cols), bf16),
            pltpu.VMEM((full, chan, cols), f32),
            pltpu.VMEM((full, chan, cols), bf16),
            pltpu.VMEM((full, chan, cols), bf16),
            pltpu.VMEM((rows, chan, cols), bf16),
            pltpu.VMEM((frames, 2, rows, chan, entries), bf16),
            pltpu.VMEM((frames, 3, rows, chan, entries), bf16),
            pltpu.VMEM((frames, 2, 2, chan, LANES), bf16),
            pltpu.VMEM((frames, 2, 2, chan, LANES), bf16),
            pltpu.VMEM((qn, chan, LANES), bf16),
            pltpu.VMEM((qn, chan, LANES), bf16),
            pltpu.VMEM((qn, chan, LANES), bf16),
            pltpu.VMEM((qn, chan, LANES), f32),
            pltpu.VMEM((qn, chan, LANES), bf16),
            pltpu.VMEM((qn, chan, LANES), bf16),
            pltpu.VMEM((per, chan, LANES), bf16),
            pltpu.VMEM((GROUPS, cols, LANES), bf16),
            pltpu.VMEM((GROUPS, LANES, cols), bf16),
            pltpu.SemaphoreType.DMA((frames,)),
            sems(2), sems(2), sems(PIECES), sems(PIECES), sems(2), sems(2),
        ],
        compiler_params=pltpu.CompilerParams(
            collective_id=0, has_side_effects=True, vmem_limit_bytes=48 * 1024 * 1024
        ),
        name="propagate",
    )(feats, send_list, recv_slot, w_unite, w_inner, w_outer, w_up)
    return out.transpose(0, 2, 1, 3)


def solution(mesh):
    placed = (
        P(None, None, "tile", "tm"),
        P(None, "tm", "tile", None, None),
        P(None, "tm", "tile", None),
        P(),
        P(),
        P(),
        P(),
    )
    return jax.shard_map(
        functools.partial(on_device, mesh.shape["tm"], mesh.shape["tile"]),
        mesh=mesh,
        in_specs=placed,
        out_specs=P(None, None, "tile", "tm"),
        check_vma=False,
    )
```

time: 59.6 us -> 65.6 us (1.10)
  Pallas kernels: 54 us -> 60.5 us
    pallas_call x1, Pallas kernels: 54 us -> 60.5 us  [on_device(): pl.pallas_call(functools.partial(kernel, n_tm, n_tile, frames, chan, rows...]
where the time goes in v1:
time: 65.6 us; the launch traced here: 65.4 us
  Pallas kernels  60.5 us (92%)
  local copies, waits for them, and re-layouts  4.82 us (7%)
    pallas_call x1, Pallas kernels, on_device(): pl.pallas_call(functools.partial(kernel, n_tm, n_tile, frames, chan, rows...  60.5 us
    unnamed x12, local copies, waits for them, and re-layouts  3.13 us
    transpose x1, local copies, waits for them, and re-layouts, on_device(): return out.transpose(0, 2, 1, 3)  1.69 us

profile of v1, /device:TPU:1, one launch (start us, length us, event | category | flops | bytes accessed | tf_op | source)
XLA Modules:
  0.0 65.4 jit_solution(16209359628191137556)
XLA Ops:
  0.0 0.7 %copy.9.list_ref = s32[4,1,1,3,8]{4,3,2,1,0:T(4,128)S(1)} copy(s32[4,1,1,3,8]{4,2,3,1,0:T(1,128)} %param.8) | data formatting | bytes 768 | tf_op args[1]
  0.7 0.0 copy-start
  0.7 0.0 copy-start.1
  0.7 0.0 copy-start.2
  0.7 0.0 copy-start.3
  0.7 0.0 copy-start.4
  0.7 2.4 %copy.12 = bf16[4,64,16,256]{3,1,2,0:T(8,128)(2,1)S(1)} copy(bf16[4,64,16,256]{3,2,1,0:T(8,128)(2,1)} %param.7) | data formatting | bytes 4194304 | tf_op args[0]
  3.1 0.0 copy-done
  3.2 0.0 copy-done.1
  3.2 0.0 copy-done.2
  3.2 0.0 copy-done.3
  3.2 0.0 copy-done.4
  3.2 60.5 %propagate.1 = bf16[4,16,48,256]{3,2,1,0:T(8,128)(2,1)S(1)} custom-call(bf16[4,16,64,256]{3,2,1,0:T(8,128)(2,1)S(1)} %bitcast.4, s32[4,1,1,3,8]{4,3,2,1,0:T(4,128)S(1)} %copy.9.list_ref, s32[4,1,1,16]{3,2,1,0:T(1,128)S(1)} %copy-done.4, bf16[3,3,64,128]{3,2,1,0:T(8,128)(2,1)S(1)} %copy-done, bf16[3,3,64,64]{3,2,1,0:T(8,128)(2,1)S(1)} %copy-done.1, ...), custom_call_target="tpu_custom_call" | custom-call | tf_op jit(solution)/shard_map/propagate/pallas_call | solution.py:370
  63.7 1.7 %copy.10 = bf16[4,48,16,256]{3,2,1,0:T(8,128)(2,1)} copy(bf16[4,48,16,256]{3,1,2,0:T(8,128)(2,1)S(1)} %bitcast.5) | data formatting | bytes 3145728 | tf_op jit(solution)/shard_map/transpose | solution.py:407
Async XLA Ops:
  0.7 2.4 %copy-start = (bf16[3,3,64,128]{3,2,1,0:T(8,128)(2,1)S(1)}, bf16[3,3,64,128]{3,2,1,0:T(8,128)(2,1)}, u32[]{:S(2)}) copy-start(bf16[3,3,64,128]{3,2,1,0:T(8,128)(2,1)} %tu_ref.1) | copy-start | bytes 442372
  0.7 2.5 %copy-start.1 = (bf16[3,3,64,64]{3,2,1,0:T(8,128)(2,1)S(1)}, bf16[3,3,64,64]{3,2,1,0:T(8,128)(2,1)}, u32[]{:S(2)}) copy-start(bf16[3,3,64,64]{3,2,1,0:T(8,128)(2,1)} %ti_ref.1) | copy-start | bytes 221188
  0.7 2.5 %copy-start.2 = (bf16[3,3,64,64]{3,2,1,0:T(8,128)(2,1)S(1)}, bf16[3,3,64,64]{3,2,1,0:T(8,128)(2,1)}, u32[]{:S(2)}) copy-start(bf16[3,3,64,64]{3,2,1,0:T(8,128)(2,1)} %to_ref.1) | copy-start | bytes 221188
  0.7 2.5 %copy-start.3 = (bf16[48,64]{1,0:T(8,128)(2,1)S(1)}, bf16[48,64]{1,0:T(8,128)(2,1)}, u32[]{:S(2)}) copy-start(bf16[48,64]{1,0:T(8,128)(2,1)} %wp_ref.1) | copy-start | bytes 18436
  0.7 2.5 %copy-start.4 = (s32[4,1,1,16]{3,2,1,0:T(1,128)S(1)}, s32[4,1,1,16]{3,2,1,0:T(1,128)}, u32[]{:S(2)}) copy-start(s32[4,1,1,16]{3,2,1,0:T(1,128)} %slot_ref.1) | copy-start | bytes 772

commit v2 on v0

--- a/solution.py
+++ b/solution.py
@@ -12,6 +12,7 @@
 GROUPS = 4
 SPAN = 32
 LANES = GROUPS * SPAN
+PIECES = 2
 bf16 = jnp.bfloat16
 f32 = jnp.float32
 
@@ -49,6 +50,7 @@
     cap = list_ref.shape[4]
     blocks = slot_ref.shape[3]
     entries = cap * rows
+    piece = rows // PIECES
 
     def load(f):
         return pltpu.make_async_copy(
@@ -129,12 +131,13 @@
                               send.at[f, 1], recv.at[f, 1], down), has_up),
         )
 
-    def block_pair(f):
+    def block_pair(f, h):
+        part = pl.ds(piece * h, piece)
         return (
-            (has_down, remote(offer.at[f, 0], pool.at[f, 0],
-                              blk_send.at[f, 0], blk_recv.at[f, 0], down), has_up),
-            (has_up, remote(offer.at[f, 1], pool.at[f, 2],
-                            blk_send.at[f, 1], blk_recv.at[f, 1], up), has_down),
+            (has_down, remote(offer.at[f, 0, part], pool.at[f, 0, part],
+                              blk_send.at[f, h, 0], blk_recv.at[f, h, 0], down), has_up),
+            (has_up, remote(offer.at[f, 1, part], pool.at[f, 2, part],
+                            blk_send.at[f, h, 1], blk_recv.at[f, h, 1], up), has_down),
         )
 
     def zone_pair(f, base, send, recv):
@@ -202,20 +205,29 @@
 
         @pl.when(f > 0)
         def _():
-            arrive(block_pair(f))
             spot = lax.broadcasted_iota(jnp.int32, (1, cols), 1)
             source = jnp.zeros((1, cols), jnp.int32)
             for d in range(blocks):
                 source = jnp.where(spot // rows == d, slot_ref[f, 0, 0, d] * rows, source)
             index = lax.broadcasted_iota(jnp.int32, (3 * entries, cols), 0)
             placer = (index == source + spot % rows).astype(f32).astype(bf16)
-            whole = jnp.concatenate([pool[f, o].reshape(rows * chan, entries) for o in range(3)], 1)
-            warped = jnp.dot(whole, placer, preferred_element_type=f32)
-            join[f, HALO : HALO + rows, 0:chan, :] = warped.astype(bf16).reshape(rows, chan, cols)
+            for h in range(PIECES):
+                arrive(block_pair(f, h))
+                part = slice(piece * h, piece * (h + 1))
+                whole = jnp.concatenate([pool[f, o, part].reshape(piece * chan, entries) for o in range(3)], 1)
+                placed = jnp.dot(whole, placer, preferred_element_type=f32).astype(bf16)
+                join[f, HALO + piece * h : HALO + piece * (h + 1), 0:chan, :] = placed.reshape(piece, chan, cols)
             start(row_pair(f, 0, wr_send, wr_recv))
 
         for r in range(HALO + 1, HALO + rows - 1):
             united[r] = unite_row(f, r).astype(bf16)
+
+        def inner_row(r):
+            slab = united[pl.ds(r - 1, 3)].reshape(3 * chan, cols)
+            return jnp.maximum(conv_slab(wi_ref[...], slab), 0.0)
+
+        for r in range(HALO + 2, HALO + rows - 2):
+            inner[r] = inner_row(r).astype(bf16)
 
         @pl.when(f > 0)
         def _():
@@ -230,11 +242,7 @@
             value = unite_row(f, r)
             united[r] = (value if r < HALO + rows else jnp.where(has_down, value, 0.0)).astype(bf16)
 
-        def inner_row(r):
-            slab = united[pl.ds(r - 1, 3)].reshape(3 * chan, cols)
-            return jnp.maximum(conv_slab(wi_ref[...], slab), 0.0)
-
-        for r in range(HALO, HALO + rows):
+        for r in (3, 4, HALO + rows - 2, HALO + rows - 1):
             inner[r] = inner_row(r).astype(bf16)
         inner[2] = jnp.where(has_up, inner_row(2), 0.0).astype(bf16)
         inner[HALO + rows] = jnp.where(has_down, inner_row(HALO + rows), 0.0).astype(bf16)
@@ -287,10 +295,13 @@
                 for c in range(cap):
                     target = jnp.where(spot // rows == c, list_ref[f + 1, 0, 0, o, c] * rows, target)
                 pickers.append((index == target + spot % rows).astype(f32).astype(bf16))
-            away = jnp.dot(whole, jnp.concatenate(pickers[:2], 1), preferred_element_type=f32).astype(bf16)
-            offer[f + 1, 0] = away[:, :entries].reshape(rows, chan, entries)
-            offer[f + 1, 1] = away[:, entries:].reshape(rows, chan, entries)
-            start(block_pair(f + 1))
+            both = jnp.concatenate(pickers[:2], 1)
+            for h in range(PIECES):
+                part = slice(piece * h, piece * (h + 1))
+                away = jnp.dot(state[part].reshape(piece * chan, cols), both, preferred_element_type=f32).astype(bf16)
+                offer[f + 1, 0, part] = away[:, :entries].reshape(piece, chan, entries)
+                offer[f + 1, 1, part] = away[:, entries:].reshape(piece, chan, entries)
+                start(block_pair(f + 1, h))
             kept = jnp.dot(whole, pickers[2], preferred_element_type=f32).astype(bf16)
             pool[f + 1, 1] = kept.reshape(rows, chan, entries)
 
@@ -304,7 +315,8 @@
         def _():
             sent(row_pair(f, 0, wr_send, wr_recv))
             sent(zone_pair(f, 0, zw_send, zw_recv))
-            sent(block_pair(f))
+            for h in range(PIECES):
+                sent(block_pair(f, h))
 
         return carry
 
@@ -348,7 +360,7 @@
             pltpu.VMEM((GROUPS, cols, LANES), bf16),
             pltpu.VMEM((GROUPS, LANES, cols), bf16),
             pltpu.SemaphoreType.DMA((frames,)),
-        ] + [sems] * 10,
+        ] + [sems] * 4 + [pltpu.SemaphoreType.DMA((frames, PIECES, 2))] * 2 + [sems] * 4,
         compiler_params=pltpu.CompilerParams(
             collective_id=0, has_side_effects=True, vmem_limit_bytes=48 * 1024 * 1024
         ),

time: 59.6 us -> 59.3 us (level)
  no operation moved by 1% of the time
where the time goes in v2:
time: 59.3 us; the launch traced here: 58.6 us
  Pallas kernels  53.7 us (91%)
  local copies, waits for them, and re-layouts  4.82 us (8%)
    pallas_call x1, Pallas kernels, on_device(): pl.pallas_call(functools.partial(kernel, n_tm, n_tile, frames, chan, rows...  53.7 us
    unnamed x12, local copies, waits for them, and re-layouts  3.13 us
    transpose x1, local copies, waits for them, and re-layouts, on_device(): return out.transpose(0, 2, 1, 3)  1.69 us

profile of v2, /device:TPU:1, one launch (start us, length us, event | category | flops | bytes accessed | tf_op | source)
XLA Modules:
  0.0 58.6 jit_solution(6204570240381277597)
XLA Ops:
  0.0 0.7 %copy.9.list_ref = s32[4,1,1,3,8]{4,3,2,1,0:T(4,128)S(1)} copy(s32[4,1,1,3,8]{4,2,3,1,0:T(1,128)} %param.8) | data formatting | bytes 768 | tf_op args[1]
  0.7 0.0 copy-start
  0.7 0.0 copy-start.1
  0.7 0.0 copy-start.2
  0.7 0.0 copy-start.3
  0.7 0.0 copy-start.4
  0.7 2.4 %copy.12 = bf16[4,64,16,256]{3,1,2,0:T(8,128)(2,1)S(1)} copy(bf16[4,64,16,256]{3,2,1,0:T(8,128)(2,1)} %param.7) | data formatting | bytes 4194304 | tf_op args[0]
  3.1 0.0 copy-done
  3.2 0.0 copy-done.1
  3.2 0.0 copy-done.2
  3.2 0.0 copy-done.3
  3.2 0.0 copy-done.4
  3.2 53.7 %propagate.1 = bf16[4,16,48,256]{3,2,1,0:T(8,128)(2,1)S(1)} custom-call(bf16[4,16,64,256]{3,2,1,0:T(8,128)(2,1)S(1)} %bitcast.4, s32[4,1,1,3,8]{4,3,2,1,0:T(4,128)S(1)} %copy.9.list_ref, s32[4,1,1,16]{3,2,1,0:T(1,128)S(1)} %copy-done.4, bf16[3,3,64,128]{3,2,1,0:T(8,128)(2,1)S(1)} %copy-done, bf16[3,3,64,64]{3,2,1,0:T(8,128)(2,1)S(1)} %copy-done.1, ...), custom_call_target="tpu_custom_call" | custom-call | tf_op jit(solution)/shard_map/propagate/pallas_call | solution.py:337
  56.9 1.7 %copy.10 = bf16[4,48,16,256]{3,2,1,0:T(8,128)(2,1)} copy(bf16[4,48,16,256]{3,1,2,0:T(8,128)(2,1)S(1)} %bitcast.5) | data formatting | bytes 3145728 | tf_op jit(solution)/shard_map/transpose | solution.py:369
Async XLA Ops:
  0.7 2.4 %copy-start = (bf16[3,3,64,128]{3,2,1,0:T(8,128)(2,1)S(1)}, bf16[3,3,64,128]{3,2,1,0:T(8,128)(2,1)}, u32[]{:S(2)}) copy-start(bf16[3,3,64,128]{3,2,1,0:T(8,128)(2,1)} %tu_ref.1) | copy-start | bytes 442372
  0.7 2.5 %copy-start.1 = (bf16[3,3,64,64]{3,2,1,0:T(8,128)(2,1)S(1)}, bf16[3,3,64,64]{3,2,1,0:T(8,128)(2,1)}, u32[]{:S(2)}) copy-start(bf16[3,3,64,64]{3,2,1,0:T(8,128)(2,1)} %ti_ref.1) | copy-start | bytes 221188
  0.7 2.5 %copy-start.2 = (bf16[3,3,64,64]{3,2,1,0:T(8,128)(2,1)S(1)}, bf16[3,3,64,64]{3,2,1,0:T(8,128)(2,1)}, u32[]{:S(2)}) copy-start(bf16[3,3,64,64]{3,2,1,0:T(8,128)(2,1)} %to_ref.1) | copy-start | bytes 221188
  0.7 2.5 %copy-start.3 = (bf16[48,64]{1,0:T(8,128)(2,1)S(1)}, bf16[48,64]{1,0:T(8,128)(2,1)}, u32[]{:S(2)}) copy-start(bf16[48,64]{1,0:T(8,128)(2,1)} %wp_ref.1) | copy-start | bytes 18436
  0.7 2.5 %copy-start.4 = (s32[4,1,1,16]{3,2,1,0:T(1,128)S(1)}, s32[4,1,1,16]{3,2,1,0:T(1,128)}, u32[]{:S(2)}) copy-start(s32[4,1,1,16]{3,2,1,0:T(1,128)} %slot_ref.1) | copy-start | bytes 772

commit v3 on v2

--- a/solution.py
+++ b/solution.py
@@ -30,6 +30,15 @@
     left = pltpu.roll(part[0:out], 1, 1)
     right = pltpu.roll(part[2 * out : 3 * out], n - 1, 1)
     return left + part[out : 2 * out] + right
+
+
+def looped(first, count, step, body):
+    def go(i, carry):
+        for k in range(step):
+            body(first + i * step + k)
+        return carry
+
+    lax.fori_loop(0, count // step, go, 0)
 
 
 def kernel(
@@ -219,15 +228,19 @@
                 join[f, HALO + piece * h : HALO + piece * (h + 1), 0:chan, :] = placed.reshape(piece, chan, cols)
             start(row_pair(f, 0, wr_send, wr_recv))
 
-        for r in range(HALO + 1, HALO + rows - 1):
+        def unite_inside(r):
             united[r] = unite_row(f, r).astype(bf16)
+
+        looped(HALO + 1, rows - 2, 7, unite_inside)
 
         def inner_row(r):
             slab = united[pl.ds(r - 1, 3)].reshape(3 * chan, cols)
             return jnp.maximum(conv_slab(wi_ref[...], slab), 0.0)
 
-        for r in range(HALO + 2, HALO + rows - 2):
+        def inner_inside(r):
             inner[r] = inner_row(r).astype(bf16)
+
+        looped(HALO + 2, rows - 4, 6, inner_inside)
 
         @pl.when(f > 0)
         def _():
@@ -251,8 +264,7 @@
             slab = inner[pl.ds(r - 1, 3)].reshape(3 * chan, cols)
             state[r - HALO] = (united[r].astype(f32) + conv_slab(wo_ref[...], slab)).astype(bf16)
 
-        for r in range(HALO, HALO + rows):
-            outer_row(r)
+        looped(HALO, rows, 8, outer_row)
 
         arrive(zone_pair(f, chan, zf_send, zf_recv))
 

time: 59.3 us -> 60.2 us (1.015)
  Pallas kernels: 53.7 us -> 55 us
    pallas_call x1, Pallas kernels: 53.7 us -> 55 us  [on_device(): pl.pallas_call(functools.partial(kernel, n_tm, n_tile, frames, chan, rows...]
where the time goes in v3:
time: 60.2 us; the launch traced here: 59.9 us
  Pallas kernels  55 us (91%)
  local copies, waits for them, and re-layouts  4.82 us (8%)
    pallas_call x1, Pallas kernels, on_device(): pl.pallas_call(functools.partial(kernel, n_tm, n_tile, frames, chan, rows...  55 us
    unnamed x12, local copies, waits for them, and re-layouts  3.13 us
    transpose x1, local copies, waits for them, and re-layouts, on_device(): return out.transpose(0, 2, 1, 3)  1.69 us

profile of v3, /device:TPU:1, one launch (start us, length us, event | category | flops | bytes accessed | tf_op | source)
XLA Modules:
  0.0 59.9 jit_solution(12787378305146719747)
XLA Ops:
  0.0 0.7 %copy.9.list_ref = s32[4,1,1,3,8]{4,3,2,1,0:T(4,128)S(1)} copy(s32[4,1,1,3,8]{4,2,3,1,0:T(1,128)} %param.8) | data formatting | bytes 768 | tf_op args[1]
  0.7 0.0 copy-start
  0.7 0.0 copy-start.1
  0.7 0.0 copy-start.2
  0.7 0.0 copy-start.3
  0.7 0.0 copy-start.4
  0.7 2.4 %copy.12 = bf16[4,64,16,256]{3,1,2,0:T(8,128)(2,1)S(1)} copy(bf16[4,64,16,256]{3,2,1,0:T(8,128)(2,1)} %param.7) | data formatting | bytes 4194304 | tf_op args[0]
  3.1 0.0 copy-done
  3.2 0.0 copy-done.1
  3.2 0.0 copy-done.2
  3.2 0.0 copy-done.3
  3.2 0.0 copy-done.4
  3.2 55.0 %propagate.1 = bf16[4,16,48,256]{3,2,1,0:T(8,128)(2,1)S(1)} custom-call(bf16[4,16,64,256]{3,2,1,0:T(8,128)(2,1)S(1)} %bitcast.4, s32[4,1,1,3,8]{4,3,2,1,0:T(4,128)S(1)} %copy.9.list_ref, s32[4,1,1,16]{3,2,1,0:T(1,128)S(1)} %copy-done.4, bf16[3,3,64,128]{3,2,1,0:T(8,128)(2,1)S(1)} %copy-done, bf16[3,3,64,64]{3,2,1,0:T(8,128)(2,1)S(1)} %copy-done.1, ...), custom_call_target="tpu_custom_call" | custom-call | tf_op jit(solution)/shard_map/propagate/pallas_call | solution.py:349
  58.2 1.7 %copy.10 = bf16[4,48,16,256]{3,2,1,0:T(8,128)(2,1)} copy(bf16[4,48,16,256]{3,1,2,0:T(8,128)(2,1)S(1)} %bitcast.5) | data formatting | bytes 3145728 | tf_op jit(solution)/shard_map/transpose | solution.py:381
Async XLA Ops:
  0.7 2.4 %copy-start = (bf16[3,3,64,128]{3,2,1,0:T(8,128)(2,1)S(1)}, bf16[3,3,64,128]{3,2,1,0:T(8,128)(2,1)}, u32[]{:S(2)}) copy-start(bf16[3,3,64,128]{3,2,1,0:T(8,128)(2,1)} %tu_ref.1) | copy-start | bytes 442372
  0.7 2.5 %copy-start.1 = (bf16[3,3,64,64]{3,2,1,0:T(8,128)(2,1)S(1)}, bf16[3,3,64,64]{3,2,1,0:T(8,128)(2,1)}, u32[]{:S(2)}) copy-start(bf16[3,3,64,64]{3,2,1,0:T(8,128)(2,1)} %ti_ref.1) | copy-start | bytes 221188
  0.7 2.5 %copy-start.2 = (bf16[3,3,64,64]{3,2,1,0:T(8,128)(2,1)S(1)}, bf16[3,3,64,64]{3,2,1,0:T(8,128)(2,1)}, u32[]{:S(2)}) copy-start(bf16[3,3,64,64]{3,2,1,0:T(8,128)(2,1)} %to_ref.1) | copy-start | bytes 221188
  0.7 2.5 %copy-start.3 = (bf16[48,64]{1,0:T(8,128)(2,1)S(1)}, bf16[48,64]{1,0:T(8,128)(2,1)}, u32[]{:S(2)}) copy-start(bf16[48,64]{1,0:T(8,128)(2,1)} %wp_ref.1) | copy-start | bytes 18436
  0.7 2.5 %copy-start.4 = (s32[4,1,1,16]{3,2,1,0:T(1,128)S(1)}, s32[4,1,1,16]{3,2,1,0:T(1,128)}, u32[]{:S(2)}) copy-start(s32[4,1,1,16]{3,2,1,0:T(1,128)} %slot_ref.1) | copy-start | bytes 772
